TPU v7x, 256 devices: a whole 4x4x8 slice. The times are simulated.
256 devices in a mesh: ctx: 32 (over z, x), head: 8 (over y, core).
Axes of the slice: x: 4, y: 4, z: 8, core: 2. Of those that a mesh axis runs over, the one named last changes fastest.
Arguments:
- queries: bfloat16 [256, 128, 128], P('head'), may hold values from -48 to 48
- keys: bfloat16 [8, 262144, 128], P('head', 'ctx'), may hold values from -6 to 6
- values: bfloat16 [8, 262144, 128], P('head', 'ctx'), may hold values from -6 to 6
- key_block_scale: float32 [8, 4096], P('head', 'ctx'), may hold values from 0.5 to 2
- value_block_scale: float32 [8, 4096], P('head', 'ctx'), may hold values from 0.5 to 2
- selection: int32 [8, 512], P('head'), may hold values from 0 to 4095, as said below
Outputs:
- attended: bfloat16 [256, 128, 128], P('ctx', 'head')
Inputs may be any that keep to these rules, and one draw needn't show every extreme that they name: `selection`: each row lists 512 distinct block numbers in increasing order. Of the blocks i * 128 to (i + 1) * 128 - 1, a row lists between 1 and 40, and exactly 40 for some i in every row.
All inputs are finite; a program needn't handle non-finite values.
Results may differ from a plain program's by a relative error of at most 0.017.
Values may be sent and summed in bfloat16 or wider, within the bound.
A program may use at most 192 MiB of HBM per device.

v0:
```python
import jax
import jax.numpy as jnp
from jax import lax
from jax.sharding import PartitionSpec as P

HEAD_SIZE = 128
BLK = 64
MOST = 40


def combined_all(array, axis, combine):
    everything = jax.tree.map(lambda part: lax.all_gather(part, axis), array)
    first = jax.tree.map(lambda part: part[0], everything)

    def step(k, so_far):
        return combine(so_far, jax.tree.map(lambda part: part[k], everything))

    return lax.fori_loop(1, lax.axis_size(axis), step, first)


def head_partials(query_rows, key_head, value_head, key_scales, value_scales, chosen, base_block):
    local_blocks = key_head.shape[0] // BLK
    per_turn = max(1, 512 // BLK)
    key_blocks = key_head.reshape(local_blocks, BLK, HEAD_SIZE)
    value_blocks = value_head.reshape(local_blocks, BLK, HEAD_SIZE)
    first = jnp.sum(chosen < base_block)
    count = jnp.sum((chosen >= base_block) & (chosen < base_block + local_blocks))
    padded = jnp.concatenate([chosen, jnp.zeros((MOST + per_turn,), jnp.int32)])
    factor = 1.0 / HEAD_SIZE**0.5
    rows = query_rows.shape[0]

    def advance(turn, carry):
        row_peak, row_total, summed = carry
        block_ids = lax.dynamic_slice_in_dim(padded, first + turn * per_turn, per_turn) - base_block
        valid = turn * per_turn + jnp.arange(per_turn) < count
        block_ids = jnp.clip(block_ids, 0, local_blocks - 1)
        key_rows = key_blocks[block_ids].reshape(per_turn * BLK, HEAD_SIZE)
        value_rows = value_blocks[block_ids].reshape(per_turn * BLK, HEAD_SIZE)
        key_factor = jnp.repeat(
            key_scales[block_ids] * factor, BLK, total_repeat_length=per_turn * BLK
        )
        value_factor = jnp.repeat(value_scales[block_ids], BLK, total_repeat_length=per_turn * BLK)
        live = jnp.repeat(valid, BLK, total_repeat_length=per_turn * BLK)
        scores = (
            lax.dot_general(
                query_rows, key_rows, (((1,), (1,)), ((), ())), preferred_element_type=jnp.float32
            )
            * key_factor
        )
        scores = jnp.where(live, scores, -1e30)
        new_peak = jnp.maximum(row_peak, jnp.max(scores, axis=1))
        prob = jnp.where(live, jnp.exp(scores - new_peak[:, None]), 0.0)
        fading = jnp.exp(row_peak - new_peak)
        row_total = row_total * fading + jnp.sum(prob, axis=1)
        weights = (prob * value_factor).astype(jnp.bfloat16)
        summed = summed * fading[:, None] + jnp.dot(
            weights, value_rows, preferred_element_type=jnp.float32
        )
        return (new_peak, row_total, summed)

    start_state = (
        jnp.full((rows,), -1e30, jnp.float32),
        jnp.zeros((rows,), jnp.float32),
        jnp.zeros((rows, HEAD_SIZE), jnp.float32),
    )
    turns = (count + per_turn - 1) // per_turn
    return lax.fori_loop(0, turns, advance, start_state)


def combine_parts(first_part, second_part):
    peak_one, total_one, summed_one = first_part
    peak_two, total_two, summed_two = second_part
    joined = jnp.maximum(peak_one, peak_two)
    fade_one = jnp.exp(peak_one - joined)
    fade_two = jnp.exp(peak_two - joined)
    total = total_one * fade_one + total_two * fade_two
    summed = summed_one * fade_one[..., None] + summed_two * fade_two[..., None]
    return (joined, total, summed)


def on_device(queries, keys, values, key_block_scale, value_block_scale, selection):
    grouped_queries = lax.all_to_all(queries, "head", split_axis=1, concat_axis=0, tiled=True)
    token_count = grouped_queries.shape[0]
    local_heads = keys.shape[0]
    group_size = grouped_queries.shape[1] // local_heads
    ctx_index = lax.axis_index("ctx")
    base_block = ctx_index * (keys.shape[1] // BLK)
    query_rows = grouped_queries.reshape(token_count * group_size, HEAD_SIZE)
    row_peak, row_total, summed = head_partials(
        query_rows,
        keys[0],
        values[0],
        key_block_scale[0],
        value_block_scale[0],
        selection[0],
        base_block,
    )
    peaks = row_peak.reshape(token_count, group_size)
    totals = row_total.reshape(token_count, group_size)
    sums = summed.reshape(token_count, group_size, HEAD_SIZE)
    row_peak = peaks
    row_total = totals
    summed = sums
    joined, total, merged = combined_all((row_peak, row_total, summed), "ctx", combine_parts)
    owned = token_count // lax.axis_size("ctx")
    offset = ctx_index * owned
    mine_sum = lax.dynamic_slice_in_dim(merged, offset, owned, 0)
    mine_total = lax.dynamic_slice_in_dim(total, offset, owned, 0)
    result = mine_sum / mine_total[..., None]
    return result.astype(jnp.bfloat16)


def solution(mesh):
    return jax.shard_map(
        on_device,
        mesh=mesh,
        in_specs=(
            P("head", None, None),
            P("head", "ctx", None),
            P("head", "ctx", None),
            P("head", "ctx"),
            P("head", "ctx"),
            P("head", None),
        ),
        out_specs=P("ctx", "head", None),
        check_vma=False,
    )
```

profile of v0, /device:TPU:48, one launch (start us, length us, event | category | flops | bytes accessed | tf_op | source)
XLA Modules:
  0.0 762.8 jit_solution(10319837981391778700)
XLA Ops:
  9.4 4.8 all-to-all-start
  15.6 11.4 %all-to-all-done = bf16[32,128,128]{2,0,1:T(8,128)(2,1)S(1)} async-done(((bf16[32,128,128]{2,0,1:T(8,128)(2,1)}), bf16[32,128,128]{2,0,1:T(8,128)(2,1)S(1)}, u32[]{:S(2)}, u32[]{:S(2)}) %all-to-all-start) | async-done | bytes 1048608 | tf_op jit(solution)/shard_map/all_to_all | solution.py:82
  27.7 96.4 %while.42 = (s32[]{:T(128)}, f32[4096]{0:T(1024)S(1)}, f32[4096]{0:T(1024)S(1)}, f32[4096,128]{1,0:T(8,128)S(1)}, s32[]{:T(128)}, /*index=5*/s32[]{:T(128)}, s32...) while((s32[]{:T(128)}, f32[4096]{0:T(1024)S(1)}, ...), condition=%wide.region_5.7_spmd, body=%wide.region_2.6_spmd.sunk | while | flops 1104189952 | bytes 31493048 | solution.py:67
  31.7 10.0 %select_select_fusion.5 = (f32[512]{0:T(512)S(1)}, f32[512]{0:T(512)S(1)}) fusion(f32[]{:T(128)} %bitcast.161, f32[]{:T(128)} %bitcast.162, f32[]{:T(128)} %bitcast.163, f32[]{:T(128)} %bitcast.164, f32[]{:T(128)} %bitcast.165, f32[]{:T(128)} %bitcast.166, f32[]{:T(128)} %bitcast.167, f32[]{:T(128)} %bitcast.168, ...), kind=kLoop, calls=%fused_computation.30.clone.1 | loop fusion | flops 15872 | bytes 6224 | tf_op jit(solution)/shard_map/while/body/jit(_take)/select_n | solution.py:42
  42.5 4.4 select_reduce_fusion.2
  63.8 10.0 %select_select_fusion.5 = (f32[512]{0:T(512)S(1)}, f32[512]{0:T(512)S(1)}) fusion(f32[]{:T(128)} %bitcast.161, f32[]{:T(128)} %bitcast.162, f32[]{:T(128)} %bitcast.163, f32[]{:T(128)} %bitcast.164, f32[]{:T(128)} %bitcast.165, f32[]{:T(128)} %bitcast.166, f32[]{:T(128)} %bitcast.167, f32[]{:T(128)} %bitcast.168, ...), kind=kLoop, calls=%fused_computation.30.clone.1 | loop fusion | flops 15872 | bytes 6224 | tf_op jit(solution)/shard_map/while/body/jit(_take)/select_n | solution.py:42
  74.7 4.4 select_reduce_fusion.2
  96.0 10.0 %select_select_fusion.5 = (f32[512]{0:T(512)S(1)}, f32[512]{0:T(512)S(1)}) fusion(f32[]{:T(128)} %bitcast.161, f32[]{:T(128)} %bitcast.162, f32[]{:T(128)} %bitcast.163, f32[]{:T(128)} %bitcast.164, f32[]{:T(128)} %bitcast.165, f32[]{:T(128)} %bitcast.166, f32[]{:T(128)} %bitcast.167, f32[]{:T(128)} %bitcast.168, ...), kind=kLoop, calls=%fused_computation.30.clone.1 | loop fusion | flops 15872 | bytes 6224 | tf_op jit(solution)/shard_map/while/body/jit(_take)/select_n | solution.py:42
  106.8 4.4 select_reduce_fusion.2
  125.7 115.3 %all_gather.10 = f32[32,256,16]{1,2,0:T(8,128)S(1)} all-gather(f32[1,256,16]{1,2,0:T(8,128)S(1)} %copy.24), channel_id=1, replica_groups=mesh['ctx'=32,'head'=8] {'ctx'}, dimensions={0}, use_global_device_ids=true | all-gather | bytes 540672 | tf_op jit(solution)/shard_map/all_gather | solution.py:12
  241.0 46.9 %all_gather.9 = f32[32,256,16]{1,2,0:T(8,128)S(1)} all-gather(f32[1,256,16]{1,2,0:T(8,128)S(1)} %copy.23), channel_id=1, replica_groups=mesh['ctx'=32,'head'=8] {'ctx'}, dimensions={0}, use_global_device_ids=true | all-gather | bytes 540672 | tf_op jit(solution)/shard_map/all_gather | solution.py:12
  287.9 338.6 %all-gather.2.cloned.1.call-done = f32[32,256,16,128]{3,2,1,0:T(8,128)} async-done(((f32[1,256,16,128]{3,2,1,0:T(8,128)}), f32[32,256,16,128]{3,2,1,0:T(8,128)}) %all-gather.2.cloned.1.call-update) | async-done | bytes 67108880 | tf_op jit(solution)/shard_map/all_gather | solution.py:12
  628.3 126.8 %while.43 = (s32[]{:T(128)}, f32[256,16]{0,1:T(8,128)S(1)}, f32[256,16]{0,1:T(8,128)S(1)}, f32[256,16,128]{2,1,0:T(8,128)S(1)}, f32[32,256,16]{1,2,0:T(8,128)S(1...) while((s32[]{:T(128)}, f32[256,16]{0,1:T(8,128)S(1)}, ...), condition=%wide.region_7.9_spmd, body=%wide.region_6.8_spmd.sunk | while | flops 1597445 | bytes 6520975 | solution.py:18
  632.6 3.8 fusion.34
  636.7 3.8 fusion.34
  640.8 3.8 fusion.34
  644.9 3.8 fusion.34
  649.0 3.8 fusion.34
  653.0 3.8 fusion.34
  657.1 3.8 fusion.34
  661.2 3.8 fusion.34
  665.3 3.8 fusion.34
  669.4 3.8 fusion.34
  673.5 3.8 fusion.34
  677.6 3.8 fusion.34
  681.7 3.8 fusion.34
  685.8 3.8 fusion.34
  689.9 3.8 fusion.34
  698.0 3.8 fusion.34
  702.1 3.8 fusion.34
  710.3 3.8 fusion.34
  714.4 3.8 fusion.34
  (194 shorter events, 112.1 us)
Async XLA Ops:
  6.5 21.1 %copy-start.3 = (s32[4,128]{1,0:T(4,128)S(1)}, s32[4,128]{1,0:T(4,128)}, u32[]{:S(2)}) copy-start(s32[4,128]{1,0:T(4,128)} %constant.330.clone.1) | copy-start | bytes 6148
  6.5 7.7 %copy-start.4 = (s32[1,512]{1,0:T(1,128)S(1)}, s32[1,512]{1,0:T(1,128)}, u32[]{:S(2)}) copy-start(s32[1,512]{1,0:T(1,128)} %param.23) | copy-start | bytes 6148
  6.5 21.1 %copy-start.1 = (f32[1,128]{1,0:T(1,128)S(1)}, f32[1,128]{1,0:T(1,128)}, u32[]{:S(2)}) copy-start(f32[1,128]{1,0:T(1,128)} %param.22) | copy-start | bytes 1540
  6.5 21.1 %copy-start = (f32[1,128]{1,0:T(1,128)S(1)}, f32[1,128]{1,0:T(1,128)}, u32[]{:S(2)}) copy-start(f32[1,128]{1,0:T(1,128)} %param.21) | copy-start | bytes 1540
  9.4 17.6 %all-to-all-start = ((bf16[32,128,128]{2,0,1:T(8,128)(2,1)}), bf16[32,128,128]{2,0,1:T(8,128)(2,1)S(1)}, u32[]{:S(2)}, u32[]{:S(2)}) async-start(bf16[32,128,128]{2,0,1:T(8,128)(2,1)} %copy.21), calls=%async_computation | async-start | bytes 2097152 | tf_op jit(solution)/shard_map/all_to_all | solution.py:82
  14.2 612.3 %all-gather.2.cloned.1.call-start = ((), (), s32[]{:S(2)}) async-start(), calls=%async_computation.1 | async-start | bytes 69206016 | tf_op jit(solution)/shard_map/all_gather | solution.py:12
  124.0 1.3 copy-start.2
Sparse Core Ops, SparseCore 0:
  125.5 500.9 all-gather.1
where the time goes:
time: 769 us; the launch traced here: 763 us
  waiting for transfers between devices  350 us (46%)
  other arithmetic  177 us (23%)
  blocking collectives  162 us (21%)
  local copies, waits for them, and re-layouts  36.2 us (5%)
  matrix products  15.4 us (2%)
  between operations  14.2 us (2%)
    all_gather x1, waiting for transfers between devices, combined_all(): everything = jax.tree.map(lambda part: lax.all_gather(part, axis), array)  339 us
    all_gather x2, blocking collectives, combined_all(): everything = jax.tree.map(lambda part: lax.all_gather(part, axis), array)  162 us
    add x31, other arithmetic, combine_parts(): summed = summed_one * fade_one[..., None] + summed_two * fade_two[..., None]  119 us
    select_n x3, other arithmetic, advance(): jnp.repeat(value_scales[block_ids], BLK, total_repeat_length=per_turn * BLK)  30.1 us
  transfers between devices with their start and end apart: 2, of which 2 were waited for; matrix products, arithmetic and copies ran while one was open for 0% of the time, Pallas kernels for 0%

commit v1 on v0

v1 whole, which is shorter than its diff:
```python
import functools

import jax
import jax.numpy as jnp
from jax import lax
from jax.experimental import pallas as pl
from jax.experimental.pallas import tpu as pltpu
from jax.sharding import PartitionSpec as P

HEAD_SIZE = 128
BLK = 64
MOST = 40
GROUP = 16
KEYS = MOST * BLK
PART = 144
NZ, NX, NY = 8, 4, 4
NSTEP = 2 * NY
ROWS = 512
KC = 512
LOG2E = 1.4426950408889634
MESH = pl.DeviceIdType.MESH


def turn_of(step):
    u = step // 2
    return u + (u // 2) * (1 - 2 * (u % 2)), step % 2


def pack(acc, peak):
    total = acc[HEAD_SIZE : HEAD_SIZE + 1]
    high = total.astype(jnp.bfloat16).astype(jnp.float32)
    row = lax.broadcasted_iota(jnp.int32, (16, acc.shape[1]), 0)
    tail = jnp.where(row == 0, peak, jnp.where(row == 1, high, jnp.where(row == 2, total - high, 0.0)))
    return acc[:HEAD_SIZE].astype(jnp.bfloat16), tail.astype(jnp.bfloat16)


def merged(parts):
    tails = [part[HEAD_SIZE:PART, :].astype(jnp.float32) for part in parts]
    peak = functools.reduce(jnp.maximum, [tail[0:1] for tail in tails])
    total = jnp.zeros_like(peak)
    summed = jnp.zeros((HEAD_SIZE, 128), jnp.float32)
    for part, tail in zip(parts, tails):
        fade = jnp.exp2(tail[0:1] - peak)
        total = total + fade * (tail[1:2] + tail[2:3])
        summed = summed + fade * part[:HEAD_SIZE, :].astype(jnp.float32)
    return summed, total, peak


def kernel(
    q_hbm, k_hbm, v_hbm, ks_ref, vs_ref, sel_ref, selv_ref, out_ref,
    kbuf, vbuf, kk, vt, qbuf, xsend, xrecv, zsend, zrecv,
    local_sem, q_send, q_recv, x_send, x_recv, z_send, z_recv,
):
    ctx = lax.axis_index("ctx")
    head = lax.axis_index("head")
    z, x = ctx // NX, ctx % NX
    y, core = head // 2, head % 2
    local_blocks = kbuf.shape[0]

    def head_at(dy, dc):
        return ((y + dy) % NY) * 2 + (core + dc) % 2

    k_copy = pltpu.make_async_copy(k_hbm, kbuf, local_sem.at[0])
    v_copy = pltpu.make_async_copy(v_hbm, vbuf, local_sem.at[1])
    k_copy.start()
    v_copy.start()
    q_copy = pltpu.make_async_copy(
        q_hbm.at[:, pl.ds(pl.multiple_of(head * GROUP, GROUP), GROUP), :], qbuf.at[0], local_sem.at[2]
    )
    q_copy.start()

    barrier = pltpu.get_barrier_semaphore()
    for step in range(1, NSTEP):
        dy, dc = turn_of(step)
        pl.semaphore_signal(barrier, inc=1, device_id=(ctx, head_at(dy, dc)), device_id_type=MESH)
    for dx in range(1, NX):
        pl.semaphore_signal(barrier, inc=1, device_id=(z * NX + (x + dx) % NX, head), device_id_type=MESH)
    for dz in range(1, NZ):
        pl.semaphore_signal(barrier, inc=1, device_id=(((z + dz) % NZ) * NX + x, head), device_id_type=MESH)
    pl.semaphore_wait(barrier, NSTEP - 1 + NX - 1 + NZ - 1)

    def q_remote(step):
        dy, dc = turn_of(step)
        to = head_at(dy, dc)
        return pltpu.make_async_remote_copy(
            src_ref=q_hbm.at[:, pl.ds(pl.multiple_of(to * GROUP, GROUP), GROUP), :],
            dst_ref=qbuf.at[step],
            send_sem=q_send.at[step],
            recv_sem=q_recv.at[step],
            device_id=(ctx, to),
            device_id_type=MESH,
        )

    for step in range(1, NSTEP):
        q_remote(step).start()

    base = ctx * local_blocks
    chosen = selv_ref[...]
    first = jnp.sum((chosen < base).astype(jnp.int32))
    upto = jnp.sum((chosen < base + local_blocks).astype(jnp.int32))
    last = upto - 1
    factor = LOG2E / HEAD_SIZE**0.5

    k_copy.wait()
    v_copy.wait()

    def gather(pair, carry):
        value_parts = []
        mask_parts = []
        for half in range(2):
            j = first + pair * 2 + half
            place = jnp.maximum(jnp.minimum(j, last), 0)
            block = jnp.clip(sel_ref[0, place] - base, 0, local_blocks - 1)
            key_rows = kbuf[block].astype(jnp.float32) * (ks_ref[0, block] * factor)
            high = key_rows.astype(jnp.bfloat16)
            low = (key_rows - high.astype(jnp.float32)).astype(jnp.bfloat16)
            row = pl.multiple_of((pair * 2 + half) * BLK, BLK)
            kk[pl.ds(row, BLK), 0:HEAD_SIZE] = high
            kk[pl.ds(row, BLK), HEAD_SIZE : 2 * HEAD_SIZE] = low
            live = jnp.where(j <= last, 1.0, 0.0)
            value_parts.append(vbuf[block].astype(jnp.float32) * (vs_ref[0, block] * live))
            mask_parts.append(live)
        values = jnp.concatenate(value_parts, axis=0).T
        column = pl.ds(pl.multiple_of(pair * 2 * BLK, 2 * BLK), 2 * BLK)
        vt[0:HEAD_SIZE, column] = values.astype(jnp.bfloat16)
        lane = lax.broadcasted_iota(jnp.int32, (16, 2 * BLK), 1)
        vt[HEAD_SIZE:PART, column] = jnp.where(lane < BLK, mask_parts[0], mask_parts[1]).astype(jnp.bfloat16)
        return carry

    lax.fori_loop(0, MOST // 2, gather, 0)

    def attend(step):
        rows = qbuf[step].reshape(ROWS, HEAD_SIZE)
        turned = rows.T
        turned = jnp.concatenate([turned, turned], axis=0)
        peak = acc = None
        for i in range(KEYS // KC):
            scores = jnp.dot(kk[i * KC : (i + 1) * KC, :], turned, preferred_element_type=jnp.float32)
            best = jnp.max(scores, axis=0, keepdims=True)
            if i > 0:
                best = jnp.maximum(peak, best)
            best = best.astype(jnp.bfloat16).astype(jnp.float32)
            prob = jnp.exp2(scores - best).astype(jnp.bfloat16)
            added = jnp.dot(vt[:, i * KC : (i + 1) * KC], prob, preferred_element_type=jnp.float32)
            acc = added if i == 0 else acc * jnp.exp2(peak - best) + added
            peak = best
        summed, tail = pack(acc, peak)
        for part in range(NX):
            xsend[step, part, 0:HEAD_SIZE, :] = summed[:, part * 128 : (part + 1) * 128]
            xsend[step, part, HEAD_SIZE:PART, :] = tail[:, part * 128 : (part + 1) * 128]

    def x_remote(step, dx):
        to = (x + dx) % NX
        return pltpu.make_async_remote_copy(
            src_ref=xsend.at[step, to],
            dst_ref=xrecv.at[step, dx - 1],
            send_sem=x_send.at[step, dx - 1],
            recv_sem=x_recv.at[step, dx - 1],
            device_id=(z * NX + to, head),
            device_id_type=MESH,
        )

    def row_of(step):
        dy, dc = turn_of(step)
        return head_at(NY - dy, dc)

    def z_remote(step):
        to = row_of(step)
        slot = (z - to + NZ) % NZ - 1
        return pltpu.make_async_remote_copy(
            src_ref=zsend.at[step],
            dst_ref=zrecv.at[slot],
            send_sem=z_send.at[step],
            recv_sem=z_recv.at[slot],
            device_id=(to * NX + x, head),
            device_id_type=MESH,
        )

    def pass_on(step):
        for dx in range(1, NX):
            x_remote(step, dx).wait_recv()
        summed, total, peak = merged([xsend.at[step, x]] + [xrecv.at[step, dx] for dx in range(NX - 1)])
        acc = jnp.concatenate([summed, total], axis=0)
        summed, tail = pack(acc, peak)
        zsend[step, 0:HEAD_SIZE, :] = summed
        zsend[step, HEAD_SIZE:PART, :] = tail

        @pl.when(row_of(step) != z)
        def _():
            z_remote(step).start()

    q_copy.wait()

    def one_step(step, carry):
        @pl.when(step > 0)
        def _():
            q_remote(step).wait_recv()

        attend(step)
        for dx in range(1, NX):
            x_remote(step, dx).start()

        @pl.when(step > 0)
        def _():
            pass_on(step - 1)

        return carry

    lax.fori_loop(0, NSTEP, one_step, 0)
    pass_on(NSTEP - 1)

    own_y = (y - z // 2 + NY) % NY
    own_u = own_y + (own_y // 2) * (1 - 2 * (own_y % 2))
    own_step = own_u * 2 + (core + z) % 2
    for slot in range(NZ - 1):
        pltpu.make_async_remote_copy(
            src_ref=zsend.at[0],
            dst_ref=zrecv.at[slot],
            send_sem=z_send.at[0],
            recv_sem=z_recv.at[slot],
            device_id=(ctx, head),
            device_id_type=MESH,
        ).wait_recv()
    summed, total, _ = merged([zsend.at[own_step]] + [zrecv.at[slot] for slot in range(NZ - 1)])
    out_ref[...] = (summed / total).T.reshape(out_ref.shape).astype(out_ref.dtype)

    def finish(step, carry):
        for dx in range(1, NX):
            x_remote(step, dx).wait_send()

        @pl.when(step > 0)
        def _():
            q_remote(step).wait_send()

        @pl.when(row_of(step) != z)
        def _():
            z_remote(step).wait_send()

        return carry

    lax.fori_loop(0, NSTEP, finish, 0)


def on_device(queries, keys, values, key_block_scale, value_block_scale, selection):
    any_space = pl.BlockSpec(memory_space=pl.ANY)
    smem = pl.BlockSpec(memory_space=pltpu.SMEM)
    vmem = pl.BlockSpec(memory_space=pltpu.VMEM)
    tokens = queries.shape[0]
    blocks = (keys.shape[1] // BLK, BLK, HEAD_SIZE)
    dma = pltpu.SemaphoreType.DMA
    return pl.pallas_call(
        kernel,
        out_shape=jax.ShapeDtypeStruct((tokens // NX, GROUP, HEAD_SIZE), jnp.bfloat16),
        in_specs=[any_space] * 3 + [smem] * 3 + [vmem],
        out_specs=vmem,
        scratch_shapes=[
            pltpu.VMEM(blocks, jnp.bfloat16),
            pltpu.VMEM(blocks, jnp.bfloat16),
            pltpu.VMEM((KEYS, 2 * HEAD_SIZE), jnp.bfloat16),
            pltpu.VMEM((PART, KEYS), jnp.bfloat16),
            pltpu.VMEM((NSTEP, tokens, GROUP, HEAD_SIZE), jnp.bfloat16),
            pltpu.VMEM((NSTEP, NX, PART, 128), jnp.bfloat16),
            pltpu.VMEM((NSTEP, NX - 1, PART, 128), jnp.bfloat16),
            pltpu.VMEM((NSTEP, PART, 128), jnp.bfloat16),
            pltpu.VMEM((NZ - 1, PART, 128), jnp.bfloat16),
            dma((3,)),
            dma((NSTEP,)),
            dma((NSTEP,)),
            dma((NSTEP, NX - 1)),
            dma((NSTEP, NX - 1)),
            dma((NSTEP,)),
            dma((NZ - 1,)),
        ],
        compiler_params=pltpu.CompilerParams(
            collective_id=0, has_side_effects=True, vmem_limit_bytes=40 << 20
        ),
    )(queries, keys.reshape(blocks), values.reshape(blocks), key_block_scale, value_block_scale, selection, selection)


def solution(mesh):
    return jax.shard_map(
        on_device,
        mesh=mesh,
        in_specs=(
            P("head", None, None),
            P("head", "ctx", None),
            P("head", "ctx", None),
            P("head", "ctx"),
            P("head", "ctx"),
            P("head", None),
        ),
        out_specs=P("ctx", "head", None),
        check_vma=False,
    )
```

time: 769 us -> 53.7 us (0.07)
  waiting for transfers between devices: 350 us -> 0 us
  other arithmetic: 177 us -> 0 us
  blocking collectives: 162 us -> 0 us
  Pallas kernels: 0 us -> 46.4 us
  local copies, waits for them, and re-layouts: 36.2 us -> 7.01 us
  matrix products: 15.4 us -> 0 us
  between operations: 14.2 us -> 0.02 us
    all_gather x1 -> x0, waiting for transfers between devices: 339 us -> none  [combined_all(): everything = jax.tree.map(lambda part: lax.all_gather(part, axis), array)]
    all_gather x2 -> x0, blocking collectives: 162 us -> none  [combined_all(): everything = jax.tree.map(lambda part: lax.all_gather(part, axis), array)]
    add x65 -> x0, other arithmetic: 120 us -> none  [the longest x31 119 us: combine_parts(): summed = summed_one * fade_one[..., None] + summed_two * fade_two[..., None]]
    pallas_call x0 -> x1, Pallas kernels: none -> 46.4 us  [on_device(): pl.pallas_call(kernel, out_shape=jax.ShapeDtypeStruct((tokens // NX, GROU...]
    select_n x9 -> x0, other arithmetic: 32.5 us -> none  [the longest x3 30.1 us: advance(): jnp.repeat(value_scales[block_ids], BLK, total_repeat_length=per_turn * BLK)]
    gather x21 -> x0, local copies, waits for them, and re-layouts: 23 us -> none  [the longest x3 6.49 us: advance(): key_rows = key_blocks[block_ids].reshape(per_turn * BLK, HEAD_SIZE)]
    dot_general x6 -> x0, matrix products: 15.4 us -> none  [the longest x3 10.8 us: advance(): jnp.dot(weights, value_rows, preferred_element_type=jnp.float32)]
    gather x6 -> x0, other arithmetic: 13.2 us -> none  [the longest x3 13.2 us: advance(): live = jnp.repeat(valid, BLK, total_repeat_length=per_turn * BLK)]
  transfers between devices with their start and end apart: 2 -> 0, of which waited for: 2 -> 0; matrix products, arithmetic and copies ran while one was open for 0% -> 0% of each run, Pallas kernels for 0% -> 0%
where the time goes in v1:
time: 53.7 us; the launch traced here: 53.5 us
  Pallas kernels  46.4 us (86%)
  local copies, waits for them, and re-layouts  7.01 us (13%)
    pallas_call x1, Pallas kernels, on_device(): pl.pallas_call(kernel, out_shape=jax.ShapeDtypeStruct((tokens // NX, GROU...  46.4 us
    unnamed x13, local copies, waits for them, and re-layouts  7.01 us

profile of v1, /device:TPU:48, one launch (start us, length us, event | category | flops | bytes accessed | tf_op | source)
XLA Modules:
  0.0 53.5 jit_solution(462413509107052541)
XLA Ops:
  0.0 0.0 copy-start
  0.0 1.6 %copy-done = bf16[1,8192,128]{2,1,0:T(8,128)(2,1)S(1)} copy-done((bf16[1,8192,128]{2,1,0:T(8,128)(2,1)S(1)}, bf16[1,8192,128]{2,1,0:T(8,128)(2,1)}, u32[]{:S(2)}) %copy-start) | copy-done | bytes 2097176
  1.6 0.0 copy-start.1
  1.6 1.6 %copy-done.1 = bf16[1,8192,128]{2,1,0:T(8,128)(2,1)S(1)} copy-done((bf16[1,8192,128]{2,1,0:T(8,128)(2,1)S(1)}, bf16[1,8192,128]{2,1,0:T(8,128)(2,1)}, u32[]{:S(2)}) %copy-start.1) | copy-done | bytes 2097176
  3.2 0.0 copy-start.2
  3.2 1.2 %copy-done.2 = bf16[32,128,128]{2,1,0:T(8,128)(2,1)S(1)} copy-done((bf16[32,128,128]{2,1,0:T(8,128)(2,1)S(1)}, bf16[32,128,128]{2,1,0:T(8,128)(2,1)}, u32[]{:S(2)}) %copy-start.2) | copy-done | bytes 1048600
  4.4 0.0 copy-start.3
  4.4 0.7 %copy-done.3 = s32[1,512]{1,0:T(1,128)S(1)} copy-done((s32[1,512]{1,0:T(1,128)S(1)}, s32[1,512]{1,0:T(1,128)}, u32[]{:S(2)}) %copy-start.3) | copy-done | bytes 2072
  5.1 0.0 copy-start.4
  5.1 0.7 %copy-done.4 = f32[1,128]{1,0:T(1,128)S(1)} copy-done((f32[1,128]{1,0:T(1,128)S(1)}, f32[1,128]{1,0:T(1,128)}, u32[]{:S(2)}) %copy-start.4) | copy-done | bytes 536
  5.7 0.0 copy-start.5
  5.7 0.7 %copy-done.5 = f32[1,128]{1,0:T(1,128)S(1)} copy-done((f32[1,128]{1,0:T(1,128)S(1)}, f32[1,128]{1,0:T(1,128)}, u32[]{:S(2)}) %copy-start.5) | copy-done | bytes 536
  6.4 46.4 %shard_map.64 = bf16[8,16,128]{2,1,0:T(8,128)(2,1)S(1)} custom-call(bf16[32,128,128]{2,1,0:T(8,128)(2,1)S(1)} %copy-done.2, bf16[128,64,128]{2,1,0:T(8,128)(2,1)S(1)} %bitcast.2, bf16[128,64,128]{2,1,0:T(8,128)(2,1)S(1)} %bitcast.3, f32[1,128]{1,0:T(1,128)S(1)} %copy-done.4, f32[1,128]{1,0:T(1,128)S(1)} %copy-done.5, s32[1,512]{1,0:T(1,128)S(1)} %copy-done.3, ...), custom_call_target="tpu_custom_call" | custom-call | tf_op jit(solution)/shard_map/pallas_call | solution.py:251
  52.8 0.6 %copy.8 = bf16[8,16,128]{2,1,0:T(8,128)(2,1)} copy(bf16[8,16,128]{2,1,0:T(8,128)(2,1)S(1)} %shard_map.64) | data formatting | bytes 65536
Async XLA Ops:
  0.0 1.6 %copy-start = (bf16[1,8192,128]{2,1,0:T(8,128)(2,1)S(1)}, bf16[1,8192,128]{2,1,0:T(8,128)(2,1)}, u32[]{:S(2)}) copy-start(bf16[1,8192,128]{2,1,0:T(8,128)(2,1)} %param.7) | copy-start | bytes 6291460
  1.6 1.6 %copy-start.1 = (bf16[1,8192,128]{2,1,0:T(8,128)(2,1)S(1)}, bf16[1,8192,128]{2,1,0:T(8,128)(2,1)}, u32[]{:S(2)}) copy-start(bf16[1,8192,128]{2,1,0:T(8,128)(2,1)} %param.8) | copy-start | bytes 6291460
  3.2 1.2 %copy-start.2 = (bf16[32,128,128]{2,1,0:T(8,128)(2,1)S(1)}, bf16[32,128,128]{2,1,0:T(8,128)(2,1)}, u32[]{:S(2)}) copy-start(bf16[32,128,128]{2,1,0:T(8,128)(2,1)} %q_hbm.1) | copy-start | bytes 3145732
  4.4 0.7 %copy-start.3 = (s32[1,512]{1,0:T(1,128)S(1)}, s32[1,512]{1,0:T(1,128)}, u32[]{:S(2)}) copy-start(s32[1,512]{1,0:T(1,128)} %selv_ref.1) | copy-start | bytes 6148
  5.1 0.7 %copy-start.4 = (f32[1,128]{1,0:T(1,128)S(1)}, f32[1,128]{1,0:T(1,128)}, u32[]{:S(2)}) copy-start(f32[1,128]{1,0:T(1,128)} %ks_ref.1) | copy-start | bytes 1540
  5.7 0.7 %copy-start.5 = (f32[1,128]{1,0:T(1,128)S(1)}, f32[1,128]{1,0:T(1,128)}, u32[]{:S(2)}) copy-start(f32[1,128]{1,0:T(1,128)} %vs_ref.1) | copy-start | bytes 1540

commit v2 on v1

v2 whole, which is shorter than its diff:
```python
import functools

import jax
import jax.numpy as jnp
from jax import lax
from jax.experimental import pallas as pl
from jax.experimental.pallas import tpu as pltpu
from jax.sharding import PartitionSpec as P

HEAD_SIZE = 128
BLK = 64
MOST = 40
GROUP = 16
KEYS = MOST * BLK
PART = 144
NZ, NX, NY = 8, 4, 4
NSTEP = 2 * NY
ROWS = 1024
KC = 512
TURNS = KEYS // KC
LOG2E = 1.4426950408889634
MESH = pl.DeviceIdType.MESH


def turn_of(step):
    u = step // 2
    return u + (u // 2) * (1 - 2 * (u % 2)), step % 2


def pack(acc, peak):
    total = acc[HEAD_SIZE : HEAD_SIZE + 1]
    high = total.astype(jnp.bfloat16).astype(jnp.float32)
    row = lax.broadcasted_iota(jnp.int32, (16, acc.shape[1]), 0)
    tail = jnp.where(row == 0, peak, jnp.where(row == 1, high, jnp.where(row == 2, total - high, 0.0)))
    return acc[:HEAD_SIZE].astype(jnp.bfloat16), tail.astype(jnp.bfloat16)


def merged(parts):
    tails = [part[HEAD_SIZE:PART, :].astype(jnp.float32) for part in parts]
    peak = functools.reduce(jnp.maximum, [tail[0:1] for tail in tails])
    total = jnp.zeros_like(peak)
    summed = jnp.zeros((HEAD_SIZE, 128), jnp.float32)
    for part, tail in zip(parts, tails):
        fade = jnp.exp2(tail[0:1] - peak)
        total = total + fade * (tail[1:2] + tail[2:3])
        summed = summed + fade * part[:HEAD_SIZE, :].astype(jnp.float32)
    return summed, total, peak


def kernel(
    q_hbm, k_hbm, v_hbm, ks_hbm, vs_hbm, sel_hbm, out_ref,
    kbuf, vbuf, kk, vt, qbuf, qt, held, xsend, xrecv, zsend, zrecv, ks_ref, vs_ref, sel_ref, selv_ref,
    local_sem, q_send, q_recv, x_send, x_recv, z_send, z_recv,
):
    ctx = lax.axis_index("ctx")
    head = lax.axis_index("head")
    z, x = ctx // NX, ctx % NX
    y, core = head // 2, head % 2
    local_blocks = kbuf.shape[0]

    def head_at(dy, dc):
        return ((y + dy) % NY) * 2 + (core + dc) % 2

    local = [
        pltpu.make_async_copy(sel_hbm, selv_ref, local_sem.at[0]),
        pltpu.make_async_copy(sel_hbm, sel_ref, local_sem.at[1]),
        pltpu.make_async_copy(ks_hbm, ks_ref, local_sem.at[2]),
        pltpu.make_async_copy(vs_hbm, vs_ref, local_sem.at[3]),
        pltpu.make_async_copy(
            q_hbm.at[:, pl.ds(pl.multiple_of(head * GROUP, GROUP), GROUP), :], qbuf.at[0], local_sem.at[4]
        ),
    ]
    half = local_blocks // 2
    for k in range(2):
        part = pl.ds(k * half, half)
        local.append(pltpu.make_async_copy(k_hbm.at[part], kbuf.at[part], local_sem.at[5 + k]))
    for k in range(2):
        part = pl.ds(k * half, half)
        local.append(pltpu.make_async_copy(v_hbm.at[part], vbuf.at[part], local_sem.at[7 + k]))
    for copy in local:
        copy.start()

    barrier = pltpu.get_barrier_semaphore()
    for step in range(1, NSTEP):
        dy, dc = turn_of(step)
        pl.semaphore_signal(barrier, inc=1, device_id=(ctx, head_at(dy, dc)), device_id_type=MESH)
    for dx in range(1, NX):
        pl.semaphore_signal(barrier, inc=1, device_id=(z * NX + (x + dx) % NX, head), device_id_type=MESH)
    for dz in range(1, NZ):
        pl.semaphore_signal(barrier, inc=1, device_id=(((z + dz) % NZ) * NX + x, head), device_id_type=MESH)
    pl.semaphore_wait(barrier, NSTEP - 1 + NX - 1 + NZ - 1)

    def q_remote(step):
        dy, dc = turn_of(step)
        to = head_at(dy, dc)
        return pltpu.make_async_remote_copy(
            src_ref=q_hbm.at[:, pl.ds(pl.multiple_of(to * GROUP, GROUP), GROUP), :],
            dst_ref=qbuf.at[step],
            send_sem=q_send.at[step],
            recv_sem=q_recv.at[step],
            device_id=(ctx, to),
            device_id_type=MESH,
        )

    for step in range(1, NSTEP):
        q_remote(step).start()

    for copy in local[:4]:
        copy.wait()
    base = ctx * local_blocks
    chosen = selv_ref[...]
    first = jnp.sum((chosen < base).astype(jnp.int32))
    last = jnp.sum((chosen < base + local_blocks).astype(jnp.int32)) - 1
    factor = LOG2E / HEAD_SIZE**0.5

    for copy in local[5:]:
        copy.wait()

    def gather(turn):
        for pair in range(turn * KC // (2 * BLK), (turn + 1) * KC // (2 * BLK)):
            value_parts = []
            mask_parts = []
            for side in range(2):
                j = first + pair * 2 + side
                place = jnp.maximum(jnp.minimum(j, last), 0)
                block = jnp.clip(sel_ref[0, place] - base, 0, local_blocks - 1)
                key_rows = kbuf[block].astype(jnp.float32) * (ks_ref[0, block] * factor)
                high = key_rows.astype(jnp.bfloat16)
                low = (key_rows - high.astype(jnp.float32)).astype(jnp.bfloat16)
                row = (pair * 2 + side) * BLK
                kk[row : row + BLK, 0:HEAD_SIZE] = high
                kk[row : row + BLK, HEAD_SIZE : 2 * HEAD_SIZE] = low
                live = jnp.where(j <= last, 1.0, 0.0)
                value_parts.append(vbuf[block].astype(jnp.float32) * (vs_ref[0, block] * live))
                mask_parts.append(live)
            values = jnp.concatenate(value_parts, axis=0).astype(jnp.bfloat16).T
            column = pl.ds(pair * 2 * BLK, 2 * BLK)
            vt[0:HEAD_SIZE, column] = values
            lane = lax.broadcasted_iota(jnp.int32, (16, 2 * BLK), 1)
            vt[HEAD_SIZE:PART, column] = jnp.where(lane < BLK, mask_parts[0], mask_parts[1]).astype(jnp.bfloat16)

    def turned(step):
        rows = qbuf[pl.ds(step * 2, 2)].reshape(ROWS, HEAD_SIZE)
        flat = rows.T
        return jnp.concatenate([flat, flat], axis=0)

    def scores_of(turn, queries):
        return jnp.dot(kk[turn * KC : (turn + 1) * KC, :], queries, preferred_element_type=jnp.float32)

    def x_remote(step, dx):
        to = (x + dx) % NX
        return pltpu.make_async_remote_copy(
            src_ref=xsend.at[step, to],
            dst_ref=xrecv.at[step, dx - 1],
            send_sem=x_send.at[step, dx - 1],
            recv_sem=x_recv.at[step, dx - 1],
            device_id=(z * NX + to, head),
            device_id_type=MESH,
        )

    def row_of(chunk):
        dy, dc = turn_of(chunk)
        return head_at(NY - dy, dc)

    def z_remote(chunk):
        to = row_of(chunk)
        slot = (z - to + NZ) % NZ - 1
        return pltpu.make_async_remote_copy(
            src_ref=zsend.at[chunk],
            dst_ref=zrecv.at[slot],
            send_sem=z_send.at[chunk],
            recv_sem=z_recv.at[slot],
            device_id=(to * NX + x, head),
            device_id_type=MESH,
        )

    def pass_on(step):
        for dx in range(1, NX):
            x_remote(step, dx).wait_recv()
        for side in range(2):
            chunk = step * 2 + side
            summed, total, peak = merged(
                [xsend.at[step, x, side]] + [xrecv.at[step, dx, side] for dx in range(NX - 1)]
            )
            summed, tail = pack(jnp.concatenate([summed, total], axis=0), peak)
            zsend[chunk, 0:HEAD_SIZE, :] = summed
            zsend[chunk, HEAD_SIZE:PART, :] = tail

            @pl.when(row_of(chunk) != z)
            def _():
                z_remote(chunk).start()

    def one_step(step, first_step, last_step):
        queries = qt[step % 2]
        scores = held[...]
        peak = acc = None
        for i in range(TURNS):
            if i < TURNS - 1:
                if first_step:
                    gather(i + 1)
                coming = scores_of(i + 1, queries)
            elif not last_step:
                for side in range(2):
                    q_remote(step * 2 + 2 + side).wait_recv()
                following = turned(step + 1)
                qt[(step + 1) % 2] = following
                held[...] = scores_of(0, following)
            best = jnp.max(scores, axis=0, keepdims=True)
            if i > 0:
                best = jnp.maximum(peak, best)
            best = best.astype(jnp.bfloat16).astype(jnp.float32)
            prob = jnp.exp2(scores - best).astype(jnp.bfloat16)
            added = jnp.dot(vt[:, i * KC : (i + 1) * KC], prob, preferred_element_type=jnp.float32)
            acc = added if i == 0 else acc * jnp.exp2(peak - best) + added
            peak = best
            scores = coming
            if i == 2 and not first_step:
                pass_on(step - 1)
        summed, tail = pack(acc, peak)
        for side in range(2):
            for part in range(NX):
                lanes = slice((side * NX + part) * 128, (side * NX + part + 1) * 128)
                xsend[step, part, side, 0:HEAD_SIZE, :] = summed[:, lanes]
                xsend[step, part, side, HEAD_SIZE:PART, :] = tail[:, lanes]
        for dx in range(1, NX):
            x_remote(step, dx).start()

    gather(0)
    local[4].wait()
    q_remote(1).wait_recv()
    queries = turned(0)
    qt[0] = queries
    held[...] = scores_of(0, queries)
    one_step(0, True, False)

    def middle(step, carry):
        one_step(step, False, False)
        return carry

    lax.fori_loop(1, NY - 1, middle, 0)
    one_step(NY - 1, False, True)
    pass_on(NY - 1)

    own_y = (y - z // 2 + NY) % NY
    own_u = own_y + (own_y // 2) * (1 - 2 * (own_y % 2))
    own_chunk = own_u * 2 + (core + z) % 2
    for slot in range(NZ - 1):
        pltpu.make_async_remote_copy(
            src_ref=zsend.at[0],
            dst_ref=zrecv.at[slot],
            send_sem=z_send.at[0],
            recv_sem=z_recv.at[slot],
            device_id=(ctx, head),
            device_id_type=MESH,
        ).wait_recv()
    summed, total, _ = merged([zsend.at[own_chunk]] + [zrecv.at[slot] for slot in range(NZ - 1)])
    out_ref[...] = (summed / total).T.reshape(out_ref.shape).astype(out_ref.dtype)

    def finish(chunk, carry):
        @pl.when(chunk < NY)
        def _():
            for dx in range(1, NX):
                x_remote(chunk, dx).wait_send()

        @pl.when(chunk > 0)
        def _():
            q_remote(chunk).wait_send()

        @pl.when(row_of(chunk) != z)
        def _():
            z_remote(chunk).wait_send()

        return carry

    lax.fori_loop(0, NSTEP, finish, 0)


def on_device(queries, keys, values, key_block_scale, value_block_scale, selection):
    hbm = pl.BlockSpec(memory_space=pltpu.HBM)
    tokens = queries.shape[0]
    blocks = (keys.shape[1] // BLK, BLK, HEAD_SIZE)
    dma = pltpu.SemaphoreType.DMA
    return pl.pallas_call(
        kernel,
        out_shape=jax.ShapeDtypeStruct((tokens // NX, GROUP, HEAD_SIZE), jnp.bfloat16),
        in_specs=[hbm] * 6,
        out_specs=pl.BlockSpec(memory_space=pltpu.VMEM),
        scratch_shapes=[
            pltpu.VMEM(blocks, jnp.bfloat16),
            pltpu.VMEM(blocks, jnp.bfloat16),
            pltpu.VMEM((KEYS, 2 * HEAD_SIZE), jnp.bfloat16),
            pltpu.VMEM((PART, KEYS), jnp.bfloat16),
            pltpu.VMEM((NSTEP, tokens, GROUP, HEAD_SIZE), jnp.bfloat16),
            pltpu.VMEM((2, 2 * HEAD_SIZE, ROWS), jnp.bfloat16),
            pltpu.VMEM((KC, ROWS), jnp.float32),
            pltpu.VMEM((NY, NX, 2, PART, 128), jnp.bfloat16),
            pltpu.VMEM((NY, NX - 1, 2, PART, 128), jnp.bfloat16),
            pltpu.VMEM((NSTEP, PART, 128), jnp.bfloat16),
            pltpu.VMEM((NZ - 1, PART, 128), jnp.bfloat16),
            pltpu.SMEM((1, keys.shape[1] // BLK), jnp.float32),
            pltpu.SMEM((1, keys.shape[1] // BLK), jnp.float32),
            pltpu.SMEM(selection.shape, jnp.int32),
            pltpu.VMEM(selection.shape, jnp.int32),
            dma((9,)),
            dma((NSTEP,)),
            dma((NSTEP,)),
            dma((NY, NX - 1)),
            dma((NY, NX - 1)),
            dma((NSTEP,)),
            dma((NZ - 1,)),
        ],
        compiler_params=pltpu.CompilerParams(
            collective_id=0, has_side_effects=True, vmem_limit_bytes=60 << 20
        ),
    )(queries, keys.reshape(blocks), values.reshape(blocks), key_block_scale, value_block_scale, selection)


def solution(mesh):
    return jax.shard_map(
        on_device,
        mesh=mesh,
        in_specs=(
            P("head", None, None),
            P("head", "ctx", None),
            P("head", "ctx", None),
            P("head", "ctx"),
            P("head", "ctx"),
            P("head", None),
        ),
        out_specs=P("ctx", "head", None),
        check_vma=False,
    )
```

time: 53.7 us -> 52.9 us (0.985)
  the two profiles are of different devices: /device:TPU:48 before, /device:TPU:17 now
where the time goes in v2:
time: 52.9 us; the launch traced here: 52.7 us
  Pallas kernels  51.4 us (97%)
  local copies, waits for them, and re-layouts  1.38 us (3%)
    pallas_call x1, Pallas kernels, on_device(): pl.pallas_call(kernel, out_shape=jax.ShapeDtypeStruct((tokens // NX, GROU...  51.4 us
    unnamed x1, local copies, waits for them, and re-layouts  1.38 us

profile of v2, /device:TPU:17, one launch (start us, length us, event | category | flops | bytes accessed | tf_op | source)
XLA Modules:
  0.0 52.7 jit_solution(4998352534630730995)
XLA Ops:
  0.0 51.4 %shard_map.64 = bf16[8,16,128]{2,1,0:T(8,128)(2,1)} custom-call(bf16[32,128,128]{2,1,0:T(8,128)(2,1)} %q_hbm.1, bf16[128,64,128]{2,1,0:T(8,128)(2,1)} %bitcast.2, bf16[128,64,128]{2,1,0:T(8,128)(2,1)} %bitcast.3, f32[1,128]{1,0:T(1,128)} %ks_hbm.1, f32[1,128]{1,0:T(1,128)} %vs_hbm.1, s32[1,512]{1,0:T(1,128)} %sel_hbm.1), custom_call_target="tpu_custom_call" | custom-call | tf_op jit(solution)/shard_map/pallas_call | solution.py:283
  51.4 1.4 %copy.8 = bf16[8,16,128]{2,1,0:T(8,128)(2,1)} copy(bf16[8,16,128]{2,1,0:T(8,128)(2,1)} %shard_map.64) | data formatting | bytes 65536

commit v3 on v2

--- a/solution.py
+++ b/solution.py
@@ -15,16 +15,20 @@
 PART = 144
 NZ, NX, NY = 8, 4, 4
 NSTEP = 2 * NY
-ROWS = 1024
-KC = 512
-TURNS = KEYS // KC
+ROWS = 512
+FIRST_KC, KC = 512, 1280
 LOG2E = 1.4426950408889634
 MESH = pl.DeviceIdType.MESH
 
 
 def turn_of(step):
-    u = step // 2
-    return u + (u // 2) * (1 - 2 * (u % 2)), step % 2
+    far, k = (step + 6) // 8, (step + 4) % 6
+    return far * (1 + 2 * (k % 3 % 2) + k % 3 // 2), far * (k // 3) + (1 - far) * step
+
+
+def step_of(dy, dc):
+    far = (dy + 3) // 4
+    return dc + far * (2 + 2 * dc + (dy // 2) * (4 - dy))
 
 
 def pack(acc, peak):
@@ -102,7 +106,7 @@
             device_id_type=MESH,
         )
 
-    for step in range(1, NSTEP):
+    for step in range(1, 4):
         q_remote(step).start()
 
     for copy in local[:4]:
@@ -117,7 +121,7 @@
         copy.wait()
 
     def gather(turn):
-        for pair in range(turn * KC // (2 * BLK), (turn + 1) * KC // (2 * BLK)):
+        for pair in range(turn * FIRST_KC // (2 * BLK), (turn + 1) * FIRST_KC // (2 * BLK)):
             value_parts = []
             mask_parts = []
             for side in range(2):
@@ -140,12 +144,11 @@
             vt[HEAD_SIZE:PART, column] = jnp.where(lane < BLK, mask_parts[0], mask_parts[1]).astype(jnp.bfloat16)
 
     def turned(step):
-        rows = qbuf[pl.ds(step * 2, 2)].reshape(ROWS, HEAD_SIZE)
-        flat = rows.T
+        flat = qbuf[step].reshape(ROWS, HEAD_SIZE).T
         return jnp.concatenate([flat, flat], axis=0)
 
-    def scores_of(turn, queries):
-        return jnp.dot(kk[turn * KC : (turn + 1) * KC, :], queries, preferred_element_type=jnp.float32)
+    def scores_of(start, keys, queries):
+        return jnp.dot(kk[start : start + keys, :], queries, preferred_element_type=jnp.float32)
 
     def x_remote(step, dx):
         to = (x + dx) % NX
@@ -158,17 +161,17 @@
             device_id_type=MESH,
         )
 
-    def row_of(chunk):
-        dy, dc = turn_of(chunk)
+    def row_of(step):
+        dy, dc = turn_of(step)
         return head_at(NY - dy, dc)
 
-    def z_remote(chunk):
-        to = row_of(chunk)
+    def z_remote(step):
+        to = row_of(step)
         slot = (z - to + NZ) % NZ - 1
         return pltpu.make_async_remote_copy(
-            src_ref=zsend.at[chunk],
+            src_ref=zsend.at[step],
             dst_ref=zrecv.at[slot],
-            send_sem=z_send.at[chunk],
+            send_sem=z_send.at[step],
             recv_sem=z_recv.at[slot],
             device_id=(to * NX + x, head),
             device_id_type=MESH,
@@ -177,73 +180,75 @@
     def pass_on(step):
         for dx in range(1, NX):
             x_remote(step, dx).wait_recv()
-        for side in range(2):
-            chunk = step * 2 + side
-            summed, total, peak = merged(
-                [xsend.at[step, x, side]] + [xrecv.at[step, dx, side] for dx in range(NX - 1)]
-            )
-            summed, tail = pack(jnp.concatenate([summed, total], axis=0), peak)
-            zsend[chunk, 0:HEAD_SIZE, :] = summed
-            zsend[chunk, HEAD_SIZE:PART, :] = tail
-
-            @pl.when(row_of(chunk) != z)
-            def _():
-                z_remote(chunk).start()
+        summed, total, peak = merged([xsend.at[step, x]] + [xrecv.at[step, dx] for dx in range(NX - 1)])
+        summed, tail = pack(jnp.concatenate([summed, total], axis=0), peak)
+        zsend[step, 0:HEAD_SIZE, :] = summed
+        zsend[step, HEAD_SIZE:PART, :] = tail
+
+        @pl.when(row_of(step) != z)
+        def _():
+            z_remote(step).start()
 
     def one_step(step, first_step, last_step):
+        keys = FIRST_KC if first_step else KC
         queries = qt[step % 2]
-        scores = held[...]
+        if first_step:
+            gather(0)
+            scores = scores_of(0, keys, queries)
+        else:
+            scores = held[...]
         peak = acc = None
-        for i in range(TURNS):
-            if i < TURNS - 1:
+        for start in range(0, KEYS, keys):
+            if start + keys < KEYS:
                 if first_step:
-                    gather(i + 1)
-                coming = scores_of(i + 1, queries)
+                    gather(start // keys + 1)
+                coming = scores_of(start + keys, keys, queries)
             elif not last_step:
-                for side in range(2):
-                    q_remote(step * 2 + 2 + side).wait_recv()
+                q_remote(step + 1).wait_recv()
                 following = turned(step + 1)
                 qt[(step + 1) % 2] = following
-                held[...] = scores_of(0, following)
+                held[...] = scores_of(0, KC, following)
             best = jnp.max(scores, axis=0, keepdims=True)
-            if i > 0:
+            if start > 0:
                 best = jnp.maximum(peak, best)
             best = best.astype(jnp.bfloat16).astype(jnp.float32)
             prob = jnp.exp2(scores - best).astype(jnp.bfloat16)
-            added = jnp.dot(vt[:, i * KC : (i + 1) * KC], prob, preferred_element_type=jnp.float32)
-            acc = added if i == 0 else acc * jnp.exp2(peak - best) + added
+            added = jnp.dot(vt[:, start : start + keys], prob, preferred_element_type=jnp.float32)
+            acc = added if start == 0 else acc * jnp.exp2(peak - best) + added
             peak = best
             scores = coming
-            if i == 2 and not first_step:
-                pass_on(step - 1)
         summed, tail = pack(acc, peak)
-        for side in range(2):
-            for part in range(NX):
-                lanes = slice((side * NX + part) * 128, (side * NX + part + 1) * 128)
-                xsend[step, part, side, 0:HEAD_SIZE, :] = summed[:, lanes]
-                xsend[step, part, side, HEAD_SIZE:PART, :] = tail[:, lanes]
+        for part in range(NX):
+            xsend[step, part, 0:HEAD_SIZE, :] = summed[:, part * 128 : (part + 1) * 128]
+            xsend[step, part, HEAD_SIZE:PART, :] = tail[:, part * 128 : (part + 1) * 128]
         for dx in range(1, NX):
             x_remote(step, dx).start()
 
-    gather(0)
     local[4].wait()
-    q_remote(1).wait_recv()
-    queries = turned(0)
-    qt[0] = queries
-    held[...] = scores_of(0, queries)
+    qt[0] = turned(0)
+    q_remote(4).start()
     one_step(0, True, False)
 
     def middle(step, carry):
+        @pl.when(step < 4)
+        def _():
+            q_remote(step + 4).start()
+
         one_step(step, False, False)
+
+        @pl.when(step > 1)
+        def _():
+            pass_on(step - 2)
+
         return carry
 
-    lax.fori_loop(1, NY - 1, middle, 0)
-    one_step(NY - 1, False, True)
-    pass_on(NY - 1)
+    lax.fori_loop(1, NSTEP - 1, middle, 0)
+    one_step(NSTEP - 1, False, True)
+    for step in range(NSTEP - 3, NSTEP):
+        pass_on(step)
 
     own_y = (y - z // 2 + NY) % NY
-    own_u = own_y + (own_y // 2) * (1 - 2 * (own_y % 2))
-    own_chunk = own_u * 2 + (core + z) % 2
+    own_step = step_of(own_y, (core + z) % 2)
     for slot in range(NZ - 1):
         pltpu.make_async_remote_copy(
             src_ref=zsend.at[0],
@@ -253,22 +258,20 @@
             device_id=(ctx, head),
             device_id_type=MESH,
         ).wait_recv()
-    summed, total, _ = merged([zsend.at[own_chunk]] + [zrecv.at[slot] for slot in range(NZ - 1)])
+    summed, total, _ = merged([zsend.at[own_step]] + [zrecv.at[slot] for slot in range(NZ - 1)])
     out_ref[...] = (summed / total).T.reshape(out_ref.shape).astype(out_ref.dtype)
 
-    def finish(chunk, carry):
-        @pl.when(chunk < NY)
-        def _():
-            for dx in range(1, NX):
-                x_remote(chunk, dx).wait_send()
-
-        @pl.when(chunk > 0)
-        def _():
-            q_remote(chunk).wait_send()
-
-        @pl.when(row_of(chunk) != z)
-        def _():
-            z_remote(chunk).wait_send()
+    def finish(step, carry):
+        for dx in range(1, NX):
+            x_remote(step, dx).wait_send()
+
+        @pl.when(step > 0)
+        def _():
+            q_remote(step).wait_send()
+
+        @pl.when(row_of(step) != z)
+        def _():
+            z_remote(step).wait_send()
 
         return carry
 
@@ -293,8 +296,8 @@
             pltpu.VMEM((NSTEP, tokens, GROUP, HEAD_SIZE), jnp.bfloat16),
             pltpu.VMEM((2, 2 * HEAD_SIZE, ROWS), jnp.bfloat16),
             pltpu.VMEM((KC, ROWS), jnp.float32),
-            pltpu.VMEM((NY, NX, 2, PART, 128), jnp.bfloat16),
-            pltpu.VMEM((NY, NX - 1, 2, PART, 128), jnp.bfloat16),
+            pltpu.VMEM((NSTEP, NX, PART, 128), jnp.bfloat16),
+            pltpu.VMEM((NSTEP, NX - 1, PART, 128), jnp.bfloat16),
             pltpu.VMEM((NSTEP, PART, 128), jnp.bfloat16),
             pltpu.VMEM((NZ - 1, PART, 128), jnp.bfloat16),
             pltpu.SMEM((1, keys.shape[1] // BLK), jnp.float32),
@@ -304,8 +307,8 @@
             dma((9,)),
             dma((NSTEP,)),
             dma((NSTEP,)),
-            dma((NY, NX - 1)),
-            dma((NY, NX - 1)),
+            dma((NSTEP, NX - 1)),
+            dma((NSTEP, NX - 1)),
             dma((NSTEP,)),
             dma((NZ - 1,)),
         ],

time: 52.9 us -> 38.9 us (0.74)
  the two profiles are of different devices: /device:TPU:17 before, /device:TPU:48 now
where the time goes in v3:
time: 38.9 us; the launch traced here: 38.5 us
  Pallas kernels  37.1 us (95%)
  local copies, waits for them, and re-layouts  1.38 us (4%)
    pallas_call x1, Pallas kernels, on_device(): pl.pallas_call(kernel, out_shape=jax.ShapeDtypeStruct((tokens // NX, GROU...  37.1 us
    unnamed x1, local copies, waits for them, and re-layouts  1.38 us

profile of v3, /device:TPU:48, one launch (start us, length us, event | category | flops | bytes accessed | tf_op | source)
XLA Modules:
  0.0 38.5 jit_solution(16751828714726376214)
XLA Ops:
  0.0 37.1 %shard_map.64 = bf16[8,16,128]{2,1,0:T(8,128)(2,1)} custom-call(bf16[32,128,128]{2,1,0:T(8,128)(2,1)} %q_hbm.1, bf16[128,64,128]{2,1,0:T(8,128)(2,1)} %bitcast.2, bf16[128,64,128]{2,1,0:T(8,128)(2,1)} %bitcast.3, f32[1,128]{1,0:T(1,128)} %ks_hbm.1, f32[1,128]{1,0:T(1,128)} %vs_hbm.1, s32[1,512]{1,0:T(1,128)} %sel_hbm.1), custom_call_target="tpu_custom_call" | custom-call | tf_op jit(solution)/shard_map/pallas_call | solution.py:286
  37.1 1.4 %copy.8 = bf16[8,16,128]{2,1,0:T(8,128)(2,1)} copy(bf16[8,16,128]{2,1,0:T(8,128)(2,1)} %shard_map.64) | data formatting | bytes 65536

commit v4 on v3

--- a/solution.py
+++ b/solution.py
@@ -61,6 +61,7 @@
     z, x = ctx // NX, ctx % NX
     y, core = head // 2, head % 2
     local_blocks = kbuf.shape[0]
+    share = q_hbm.shape[0] // 4
 
     def head_at(dy, dc):
         return ((y + dy) % NY) * 2 + (core + dc) % 2
@@ -94,20 +95,58 @@
         pl.semaphore_signal(barrier, inc=1, device_id=(((z + dz) % NZ) * NX + x, head), device_id_type=MESH)
     pl.semaphore_wait(barrier, NSTEP - 1 + NX - 1 + NZ - 1)
 
-    def q_remote(step):
+    def label_at(turn):
+        return turn + turn // 6 * core * (13 - 2 * turn)
+
+    def q_mate():
+        to = head_at(0, 1)
+        return pltpu.make_async_remote_copy(
+            src_ref=q_hbm.at[:, pl.ds(pl.multiple_of(to * GROUP, GROUP), GROUP), :],
+            dst_ref=qbuf.at[1],
+            send_sem=q_send.at[0, 0],
+            recv_sem=q_recv.at[0, 0],
+            device_id=(ctx, to),
+            device_id_type=MESH,
+        )
+
+    def quarter(k):
+        return pl.ds((z + k) % 4 * share, share)
+
+    def q_direct(step, k):
         dy, dc = turn_of(step)
         to = head_at(dy, dc)
         return pltpu.make_async_remote_copy(
-            src_ref=q_hbm.at[:, pl.ds(pl.multiple_of(to * GROUP, GROUP), GROUP), :],
-            dst_ref=qbuf.at[step],
-            send_sem=q_send.at[step],
-            recv_sem=q_recv.at[step],
+            src_ref=q_hbm.at[quarter(k), pl.ds(pl.multiple_of(to * GROUP, GROUP), GROUP), :],
+            dst_ref=qbuf.at[step, quarter(k)],
+            send_sem=q_send.at[step, k],
+            recv_sem=q_recv.at[step, k],
             device_id=(ctx, to),
             device_id_type=MESH,
         )
 
-    for step in range(1, 4):
-        q_remote(step).start()
+    def q_relay(step, k):
+        to = (z + 1 + k * (NZ - 2)) % NZ
+        return pltpu.make_async_remote_copy(
+            src_ref=qbuf.at[step, quarter(k)],
+            dst_ref=qbuf.at[step, quarter(k)],
+            send_sem=q_send.at[step, 2 + k],
+            recv_sem=q_recv.at[step, 2 + k],
+            device_id=(to * NX + x, head),
+            device_id_type=MESH,
+        )
+
+    def fetch(step):
+        for k in range(2):
+            q_direct(step, k).start()
+
+    def forward(step):
+        for k in range(2):
+            q_direct(step, k).wait_recv()
+            q_relay(step, k).start()
+
+    q_mate().start()
+    fetch(2)
+    fetch(3)
 
     for copy in local[:4]:
         copy.wait()
@@ -189,9 +228,10 @@
         def _():
             z_remote(step).start()
 
-    def one_step(step, first_step, last_step):
+    def one_step(turn, first_step, last_step):
+        step = label_at(turn)
         keys = FIRST_KC if first_step else KC
-        queries = qt[step % 2]
+        queries = qt[turn % 2]
         if first_step:
             gather(0)
             scores = scores_of(0, keys, queries)
@@ -202,11 +242,18 @@
             if start + keys < KEYS:
                 if first_step:
                     gather(start // keys + 1)
+                    if start == 2 * keys:
+                        fetch(4)
                 coming = scores_of(start + keys, keys, queries)
             elif not last_step:
-                q_remote(step + 1).wait_recv()
-                following = turned(step + 1)
-                qt[(step + 1) % 2] = following
+                after = label_at(turn + 1)
+                if first_step:
+                    q_mate().wait_recv()
+                else:
+                    for k in range(2):
+                        q_relay(after, k).wait_recv()
+                following = turned(after)
+                qt[(turn + 1) % 2] = following
                 held[...] = scores_of(0, KC, following)
             best = jnp.max(scores, axis=0, keepdims=True)
             if start > 0:
@@ -217,6 +264,8 @@
             acc = added if start == 0 else acc * jnp.exp2(peak - best) + added
             peak = best
             scores = coming
+            if last_step and start == 0:
+                pass_on(label_at(turn - 2))
         summed, tail = pack(acc, peak)
         for part in range(NX):
             xsend[step, part, 0:HEAD_SIZE, :] = summed[:, part * 128 : (part + 1) * 128]
@@ -226,26 +275,39 @@
 
     local[4].wait()
     qt[0] = turned(0)
-    q_remote(4).start()
     one_step(0, True, False)
-
-    def middle(step, carry):
-        @pl.when(step < 4)
-        def _():
-            q_remote(step + 4).start()
-
-        one_step(step, False, False)
-
-        @pl.when(step > 1)
-        def _():
-            pass_on(step - 2)
+    fetch(5)
+    fetch(6)
+    forward(2)
+    forward(3)
+
+    def middle(turn, carry):
+        one_step(turn, False, False)
+
+        @pl.when(turn == 1)
+        def _():
+            fetch(7)
+            forward(4)
+
+        @pl.when(turn == 2)
+        def _():
+            forward(5)
+            forward(6)
+
+        @pl.when(turn == 3)
+        def _():
+            forward(7)
+
+        @pl.when(turn > 1)
+        def _():
+            pass_on(label_at(turn - 2))
 
         return carry
 
     lax.fori_loop(1, NSTEP - 1, middle, 0)
     one_step(NSTEP - 1, False, True)
-    for step in range(NSTEP - 3, NSTEP):
-        pass_on(step)
+    for turn in range(NSTEP - 2, NSTEP):
+        pass_on(label_at(turn))
 
     own_y = (y - z // 2 + NY) % NY
     own_step = step_of(own_y, (core + z) % 2)
@@ -261,13 +323,17 @@
     summed, total, _ = merged([zsend.at[own_step]] + [zrecv.at[slot] for slot in range(NZ - 1)])
     out_ref[...] = (summed / total).T.reshape(out_ref.shape).astype(out_ref.dtype)
 
+    q_mate().wait_send()
+
     def finish(step, carry):
         for dx in range(1, NX):
             x_remote(step, dx).wait_send()
 
-        @pl.when(step > 0)
-        def _():
-            q_remote(step).wait_send()
+        @pl.when(step > 1)
+        def _():
+            for k in range(2):
+                q_direct(step, k).wait_send()
+                q_relay(step, k).wait_send()
 
         @pl.when(row_of(step) != z)
         def _():
@@ -305,8 +371,8 @@
             pltpu.SMEM(selection.shape, jnp.int32),
             pltpu.VMEM(selection.shape, jnp.int32),
             dma((9,)),
-            dma((NSTEP,)),
-            dma((NSTEP,)),
+            dma((NSTEP, 4)),
+            dma((NSTEP, 4)),
             dma((NSTEP, NX - 1)),
             dma((NSTEP, NX - 1)),
             dma((NSTEP,)),

time: 38.9 us -> 42.1 us (1.082)
  Pallas kernels: 37.1 us -> 40.4 us
    pallas_call x1, Pallas kernels: 37.1 us -> 40.4 us  [on_device(): pl.pallas_call(kernel, out_shape=jax.ShapeDtypeStruct((tokens // NX, GROU...]
where the time goes in v4:
time: 42.1 us; the launch traced here: 41.8 us
  Pallas kernels  40.4 us (96%)
  local copies, waits for them, and re-layouts  1.38 us (3%)
    pallas_call x1, Pallas kernels, on_device(): pl.pallas_call(kernel, out_shape=jax.ShapeDtypeStruct((tokens // NX, GROU...  40.4 us
    unnamed x1, local copies, waits for them, and re-layouts  1.38 us

profile of v4, /device:TPU:48, one launch (start us, length us, event | category | flops | bytes accessed | tf_op | source)
XLA Modules:
  0.0 41.8 jit_solution(1114593721832962652)
XLA Ops:
  0.0 40.4 %shard_map.64 = bf16[8,16,128]{2,1,0:T(8,128)(2,1)} custom-call(bf16[32,128,128]{2,1,0:T(8,128)(2,1)} %q_hbm.1, bf16[128,64,128]{2,1,0:T(8,128)(2,1)} %bitcast.2, bf16[128,64,128]{2,1,0:T(8,128)(2,1)} %bitcast.3, f32[1,128]{1,0:T(1,128)} %ks_hbm.1, f32[1,128]{1,0:T(1,128)} %vs_hbm.1, s32[1,512]{1,0:T(1,128)} %sel_hbm.1), custom_call_target="tpu_custom_call" | custom-call | tf_op jit(solution)/shard_map/pallas_call | solution.py:352
  40.4 1.4 %copy.8 = bf16[8,16,128]{2,1,0:T(8,128)(2,1)} copy(bf16[8,16,128]{2,1,0:T(8,128)(2,1)} %shard_map.64) | data formatting | bytes 65536

commit v5 on v3

--- a/solution.py
+++ b/solution.py
@@ -53,7 +53,7 @@
 
 def kernel(
     q_hbm, k_hbm, v_hbm, ks_hbm, vs_hbm, sel_hbm, out_ref,
-    kbuf, vbuf, kk, vt, qbuf, qt, held, xsend, xrecv, zsend, zrecv, ks_ref, vs_ref, sel_ref, selv_ref,
+    kbuf, vbuf, kk, vt, qbuf, xsend, xrecv, zsend, zrecv, ks_ref, vs_ref, sel_ref, selv_ref,
     local_sem, q_send, q_recv, x_send, x_recv, z_send, z_recv,
 ):
     ctx = lax.axis_index("ctx")
@@ -189,25 +189,18 @@
         def _():
             z_remote(step).start()
 
-    def one_step(step, first_step, last_step):
+    def one_step(step, first_step):
         keys = FIRST_KC if first_step else KC
-        queries = qt[step % 2]
+        queries = turned(step)
         if first_step:
             gather(0)
-            scores = scores_of(0, keys, queries)
-        else:
-            scores = held[...]
+        scores = scores_of(0, keys, queries)
         peak = acc = None
         for start in range(0, KEYS, keys):
             if start + keys < KEYS:
                 if first_step:
                     gather(start // keys + 1)
                 coming = scores_of(start + keys, keys, queries)
-            elif not last_step:
-                q_remote(step + 1).wait_recv()
-                following = turned(step + 1)
-                qt[(step + 1) % 2] = following
-                held[...] = scores_of(0, KC, following)
             best = jnp.max(scores, axis=0, keepdims=True)
             if start > 0:
                 best = jnp.maximum(peak, best)
@@ -225,16 +218,16 @@
             x_remote(step, dx).start()
 
     local[4].wait()
-    qt[0] = turned(0)
     q_remote(4).start()
-    one_step(0, True, False)
-
-    def middle(step, carry):
+    one_step(0, True)
+
+    def later(step, carry):
         @pl.when(step < 4)
         def _():
             q_remote(step + 4).start()
 
-        one_step(step, False, False)
+        q_remote(step).wait_recv()
+        one_step(step, False)
 
         @pl.when(step > 1)
         def _():
@@ -242,9 +235,8 @@
 
         return carry
 
-    lax.fori_loop(1, NSTEP - 1, middle, 0)
-    one_step(NSTEP - 1, False, True)
-    for step in range(NSTEP - 3, NSTEP):
+    lax.fori_loop(1, NSTEP, later, 0)
+    for step in range(NSTEP - 2, NSTEP):
         pass_on(step)
 
     own_y = (y - z // 2 + NY) % NY
@@ -294,8 +286,6 @@
             pltpu.VMEM((KEYS, 2 * HEAD_SIZE), jnp.bfloat16),
             pltpu.VMEM((PART, KEYS), jnp.bfloat16),
             pltpu.VMEM((NSTEP, tokens, GROUP, HEAD_SIZE), jnp.bfloat16),
-            pltpu.VMEM((2, 2 * HEAD_SIZE, ROWS), jnp.bfloat16),
-            pltpu.VMEM((KC, ROWS), jnp.float32),
             pltpu.VMEM((NSTEP, NX, PART, 128), jnp.bfloat16),
             pltpu.VMEM((NSTEP, NX - 1, PART, 128), jnp.bfloat16),
             pltpu.VMEM((NSTEP, PART, 128), jnp.bfloat16),

time: 38.9 us -> 38 us (0.977)
  Pallas kernels: 37.1 us -> 36.5 us
    pallas_call x1, Pallas kernels: 37.1 us -> 36.5 us  [on_device(): pl.pallas_call(kernel, out_shape=jax.ShapeDtypeStruct((tokens // NX, GROU...]
where the time goes in v5:
time: 38 us; the launch traced here: 37.8 us
  Pallas kernels  36.5 us (96%)
  local copies, waits for them, and re-layouts  1.38 us (4%)
    pallas_call x1, Pallas kernels, on_device(): pl.pallas_call(kernel, out_shape=jax.ShapeDtypeStruct((tokens // NX, GROU...  36.5 us
    unnamed x1, local copies, waits for them, and re-layouts  1.38 us

profile of v5, /device:TPU:48, one launch (start us, length us, event | category | flops | bytes accessed | tf_op | source)
XLA Modules:
  0.0 37.8 jit_solution(9854355912257306981)
XLA Ops:
  0.0 36.5 %shard_map.64 = bf16[8,16,128]{2,1,0:T(8,128)(2,1)} custom-call(bf16[32,128,128]{2,1,0:T(8,128)(2,1)} %q_hbm.1, bf16[128,64,128]{2,1,0:T(8,128)(2,1)} %bitcast.2, bf16[128,64,128]{2,1,0:T(8,128)(2,1)} %bitcast.3, f32[1,128]{1,0:T(1,128)} %ks_hbm.1, f32[1,128]{1,0:T(1,128)} %vs_hbm.1, s32[1,512]{1,0:T(1,128)} %sel_hbm.1), custom_call_target="tpu_custom_call" | custom-call | tf_op jit(solution)/shard_map/pallas_call | solution.py:278
  36.5 1.4 %copy.8 = bf16[8,16,128]{2,1,0:T(8,128)(2,1)} copy(bf16[8,16,128]{2,1,0:T(8,128)(2,1)} %shard_map.64) | data formatting | bytes 65536

commit v6 on v5

--- a/solution.py
+++ b/solution.py
@@ -64,6 +64,25 @@
 
     def head_at(dy, dc):
         return ((y + dy) % NY) * 2 + (core + dc) % 2
+
+    barrier = pltpu.get_barrier_semaphore()
+
+    def greet(to):
+        pl.semaphore_signal(barrier, inc=1, device_id=to, device_id_type=MESH)
+
+    for dz in (4, 3, 5, 2, 6):
+        greet((((z + dz) % NZ) * NX + x, head))
+    for step in (4, 7):
+        dy, dc = turn_of(step)
+        greet((ctx, head_at(dy, dc)))
+    greet((z * NX + (x + 2) % NX, head))
+    for step in (2, 3, 5, 6, 1):
+        dy, dc = turn_of(step)
+        greet((ctx, head_at(dy, dc)))
+    for dx in (1, 3):
+        greet((z * NX + (x + dx) % NX, head))
+    for dz in (1, 7):
+        greet((((z + dz) % NZ) * NX + x, head))
 
     local = [
         pltpu.make_async_copy(sel_hbm, selv_ref, local_sem.at[0]),
@@ -84,14 +103,6 @@
     for copy in local:
         copy.start()
 
-    barrier = pltpu.get_barrier_semaphore()
-    for step in range(1, NSTEP):
-        dy, dc = turn_of(step)
-        pl.semaphore_signal(barrier, inc=1, device_id=(ctx, head_at(dy, dc)), device_id_type=MESH)
-    for dx in range(1, NX):
-        pl.semaphore_signal(barrier, inc=1, device_id=(z * NX + (x + dx) % NX, head), device_id_type=MESH)
-    for dz in range(1, NZ):
-        pl.semaphore_signal(barrier, inc=1, device_id=(((z + dz) % NZ) * NX + x, head), device_id_type=MESH)
     pl.semaphore_wait(barrier, NSTEP - 1 + NX - 1 + NZ - 1)
 
     def q_remote(step):
@@ -214,17 +225,20 @@
         for part in range(NX):
             xsend[step, part, 0:HEAD_SIZE, :] = summed[:, part * 128 : (part + 1) * 128]
             xsend[step, part, HEAD_SIZE:PART, :] = tail[:, part * 128 : (part + 1) * 128]
-        for dx in range(1, NX):
+        for dx in (2, 1, 3):
             x_remote(step, dx).start()
 
     local[4].wait()
-    q_remote(4).start()
     one_step(0, True)
 
     def later(step, carry):
         @pl.when(step < 4)
         def _():
-            q_remote(step + 4).start()
+            q_remote(step + 3 + step // 3).start()
+
+        @pl.when(step == 2)
+        def _():
+            q_remote(6).start()
 
         q_remote(step).wait_recv()
         one_step(step, False)

time: 38 us -> 36.8 us (0.968)
  Pallas kernels: 36.5 us -> 35.3 us
    pallas_call x1, Pallas kernels: 36.5 us -> 35.3 us  [on_device(): pl.pallas_call(kernel, out_shape=jax.ShapeDtypeStruct((tokens // NX, GROU...]
where the time goes in v6:
time: 36.8 us; the launch traced here: 36.7 us
  Pallas kernels  35.3 us (96%)
  local copies, waits for them, and re-layouts  1.38 us (4%)
    pallas_call x1, Pallas kernels, on_device(): pl.pallas_call(kernel, out_shape=jax.ShapeDtypeStruct((tokens // NX, GROU...  35.3 us
    unnamed x1, local copies, waits for them, and re-layouts  1.38 us

profile of v6, /device:TPU:48, one launch (start us, length us, event | category | flops | bytes accessed | tf_op | source)
XLA Modules:
  0.0 36.7 jit_solution(16986489296529834424)
XLA Ops:
  0.0 35.3 %shard_map.64 = bf16[8,16,128]{2,1,0:T(8,128)(2,1)} custom-call(bf16[32,128,128]{2,1,0:T(8,128)(2,1)} %q_hbm.1, bf16[128,64,128]{2,1,0:T(8,128)(2,1)} %bitcast.2, bf16[128,64,128]{2,1,0:T(8,128)(2,1)} %bitcast.3, f32[1,128]{1,0:T(1,128)} %ks_hbm.1, f32[1,128]{1,0:T(1,128)} %vs_hbm.1, s32[1,512]{1,0:T(1,128)} %sel_hbm.1), custom_call_target="tpu_custom_call" | custom-call | tf_op jit(solution)/shard_map/pallas_call | solution.py:292
  35.3 1.4 %copy.8 = bf16[8,16,128]{2,1,0:T(8,128)(2,1)} copy(bf16[8,16,128]{2,1,0:T(8,128)(2,1)} %shard_map.64) | data formatting | bytes 65536

commit v7 on v6

--- a/solution.py
+++ b/solution.py
@@ -243,14 +243,14 @@
         q_remote(step).wait_recv()
         one_step(step, False)
 
-        @pl.when(step > 1)
-        def _():
-            pass_on(step - 2)
+        @pl.when(step > 2)
+        def _():
+            pass_on(step - 3)
 
         return carry
 
     lax.fori_loop(1, NSTEP, later, 0)
-    for step in range(NSTEP - 2, NSTEP):
+    for step in range(NSTEP - 3, NSTEP):
         pass_on(step)
 
     own_y = (y - z // 2 + NY) % NY

time: 36.8 us -> 36.8 us (level)
  no operation moved by 1% of the time
where the time goes in v7:
time: 36.8 us; the launch traced here: 36.6 us
  Pallas kernels  35.3 us (96%)
  local copies, waits for them, and re-layouts  1.38 us (4%)
    pallas_call x1, Pallas kernels, on_device(): pl.pallas_call(kernel, out_shape=jax.ShapeDtypeStruct((tokens // NX, GROU...  35.3 us
    unnamed x1, local copies, waits for them, and re-layouts  1.38 us

profile of v7, /device:TPU:48, one launch (start us, length us, event | category | flops | bytes accessed | tf_op | source)
XLA Modules:
  0.0 36.6 jit_solution(9993379983489611812)
XLA Ops:
  0.0 35.3 %shard_map.64 = bf16[8,16,128]{2,1,0:T(8,128)(2,1)} custom-call(bf16[32,128,128]{2,1,0:T(8,128)(2,1)} %q_hbm.1, bf16[128,64,128]{2,1,0:T(8,128)(2,1)} %bitcast.2, bf16[128,64,128]{2,1,0:T(8,128)(2,1)} %bitcast.3, f32[1,128]{1,0:T(1,128)} %ks_hbm.1, f32[1,128]{1,0:T(1,128)} %vs_hbm.1, s32[1,512]{1,0:T(1,128)} %sel_hbm.1), custom_call_target="tpu_custom_call" | custom-call | tf_op jit(solution)/shard_map/pallas_call | solution.py:292
  35.3 1.4 %copy.8 = bf16[8,16,128]{2,1,0:T(8,128)(2,1)} copy(bf16[8,16,128]{2,1,0:T(8,128)(2,1)} %shard_map.64) | data formatting | bytes 65536

commit v8 on v7

--- a/solution.py
+++ b/solution.py
@@ -232,13 +232,9 @@
     one_step(0, True)
 
     def later(step, carry):
-        @pl.when(step < 4)
-        def _():
-            q_remote(step + 3 + step // 3).start()
-
-        @pl.when(step == 2)
-        def _():
-            q_remote(6).start()
+        @pl.when(step < 5)
+        def _():
+            q_remote(step + 3).start()
 
         q_remote(step).wait_recv()
         one_step(step, False)

time: 36.8 us -> 36.8 us (level)
  no operation moved by 1% of the time
where the time goes in v8:
time: 36.8 us; the launch traced here: 36.7 us
  Pallas kernels  35.3 us (96%)
  local copies, waits for them, and re-layouts  1.38 us (4%)
    pallas_call x1, Pallas kernels, on_device(): pl.pallas_call(kernel, out_shape=jax.ShapeDtypeStruct((tokens // NX, GROU...  35.3 us
    unnamed x1, local copies, waits for them, and re-layouts  1.38 us

profile of v8, /device:TPU:48, one launch (start us, length us, event | category | flops | bytes accessed | tf_op | source)
XLA Modules:
  0.0 36.7 jit_solution(3206609870778463613)
XLA Ops:
  0.0 35.3 %shard_map.64 = bf16[8,16,128]{2,1,0:T(8,128)(2,1)} custom-call(bf16[32,128,128]{2,1,0:T(8,128)(2,1)} %q_hbm.1, bf16[128,64,128]{2,1,0:T(8,128)(2,1)} %bitcast.2, bf16[128,64,128]{2,1,0:T(8,128)(2,1)} %bitcast.3, f32[1,128]{1,0:T(1,128)} %ks_hbm.1, f32[1,128]{1,0:T(1,128)} %vs_hbm.1, s32[1,512]{1,0:T(1,128)} %sel_hbm.1), custom_call_target="tpu_custom_call" | custom-call | tf_op jit(solution)/shard_map/pallas_call | solution.py:288
  35.3 1.4 %copy.8 = bf16[8,16,128]{2,1,0:T(8,128)(2,1)} copy(bf16[8,16,128]{2,1,0:T(8,128)(2,1)} %shard_map.64) | data formatting | bytes 65536
